TPU v7x, 512 devices: a whole 4x4x16 slice. The times are simulated.
512 devices in a mesh: patch: 32 (over y_lo, z), head: 16 (over y_hi, x, core).
Axes of the slice: x: 4, y: 4 (y_hi: 2, y_lo: 2; y = y_hi * 2 + y_lo), z: 16, core: 2. Of those that a mesh axis runs over, the one named last changes fastest.
Arguments:
- queries: bfloat16 [3072, 8192], P('head', 'patch'), may hold values from -8 to 8
- fresh_kv: bfloat16 [8192, 48, 128], P('patch', 'head'), may hold values from -8 to 8
- stale_kv: bfloat16 [8192, 48, 128], P('patch', 'head'), may hold values from -8 to 8
- residual: bfloat16 [3072, 8192], P('head', 'patch'), may hold values from -6 to 6
- gate: float32 [3072], P('head'), may hold values from 0.5 to 2
- w_out: bfloat16 [3072, 3072], P('head'), may hold values from -0.109375 to 0.109375
Outputs:
- block_out: bfloat16 [3072, 8192], P('head', 'patch')
All inputs are finite; a program needn't handle non-finite values.
Results may differ from a plain program's by a relative error of at most 0.0065.
Values may be sent and summed in bfloat16 or wider, within the bound.
A program may use at most 64 MiB of HBM per device.

v0:
```python
import math

import jax
import jax.numpy as jnp
from jax import lax
from jax.sharding import PartitionSpec as P


def on_device(queries, fresh_kv, stale_kv, residual, gate, w_out):
    tok_count = queries.shape[1]
    head_count = fresh_kv.shape[1]
    width = fresh_kv.shape[2] // 2
    own_index = lax.axis_index("patch")
    own_offset = own_index * tok_count
    score_scale = 1.0 / math.sqrt(width)
    query_heads = queries.reshape(head_count, width, tok_count)

    def attend(carry, key_block):
        top_now, total_now, accum = carry
        key_part = key_block[:, :, :width]
        value_part = key_block[:, :, width:]
        scores = (
            jnp.einsum("hdi,jhd->hij", query_heads, key_part, preferred_element_type=jnp.float32)
            * score_scale
        )
        new_top = jnp.maximum(top_now, jnp.max(scores, axis=2))
        weights_exp = jnp.exp(scores - new_top[:, :, None])
        rescale = jnp.exp(top_now - new_top)
        total_now = total_now * rescale + jnp.sum(weights_exp, axis=2)
        probs = weights_exp.astype(jnp.bfloat16)
        accum = accum * rescale[:, None, :] + jnp.einsum(
            "hij,jhd->hdi", probs, value_part, preferred_element_type=jnp.float32
        )
        return (new_top, total_now, accum)

    initial = (
        jnp.full((head_count, tok_count), -1e30, jnp.float32),
        jnp.zeros((head_count, tok_count), jnp.float32),
        jnp.zeros((head_count, width, tok_count), jnp.float32),
    )
    gathered = lax.all_gather(stale_kv, "patch", axis=0, tiled=True)
    merged = lax.dynamic_update_slice(gathered, fresh_kv, (own_offset, jnp.int32(0), jnp.int32(0)))
    row_count = merged.shape[0]
    block_rows = math.gcd(row_count, 2048)
    stacked = merged.reshape(row_count // block_rows, block_rows, head_count, 2 * width)

    def step_fn(state, index_block):
        index, key_block = index_block
        return (attend(state, key_block), None)

    indices = jnp.arange(row_count // block_rows, dtype=jnp.int32)
    result, unused = lax.scan(step_fn, initial, (indices, stacked))
    final = result
    top_now, total_now, accum = final
    attended = (
        (accum / total_now[:, None, :]).astype(jnp.bfloat16).reshape(head_count * width, tok_count)
    )
    all_heads = lax.all_gather(attended, "head", axis=0, tiled=True)
    projected = jnp.dot(w_out, all_heads, preferred_element_type=jnp.float32)
    result = residual.astype(jnp.float32) + gate[:, None] * projected
    return result.astype(jnp.bfloat16)


def solution(mesh):
    placed = (
        P("head", "patch"),
        P("patch", "head", None),
        P("patch", "head", None),
        P("head", "patch"),
        P("head"),
        P("head", None),
    )
    return jax.shard_map(
        on_device, mesh=mesh, in_specs=placed, out_specs=P("head", "patch"), check_vma=False
    )
```

profile of v0, /device:TPU:1, one launch (start us, length us, event | category | flops | bytes accessed | tf_op | source)
XLA Modules:
  0.0 258.1 jit_solution(9705198429377723539)
XLA Ops:
  6.5 0.0 copy-start
  6.5 0.0 all-gather.3.cloned.1.call-start
  6.5 0.7 all-gather.3.cloned.1.call-update
  7.3 0.0 all-gather.5.cloned.1.call-start
  7.3 131.6 %all-gather.3.cloned.1.call-done = bf16[8192,3,128]{2,0,1:T(8,128)(2,1)} async-done(((bf16[256,3,128]{2,0,1:T(8,128)(2,1)}), bf16[8192,3,128]{2,0,1:T(8,128)(2,1)}) %all-gather.3.cloned.1.call-update) | async-done | bytes 6291472 | tf_op jit(solution)/shard_map/all_gather | solution.py:41
  138.9 1.6 constant_dynamic-update-slice_fusion
  140.5 0.0 copy-start.2
  140.5 0.0 copy-start.3
  140.5 31.0 %while.15 = (s32[]{:T(128)}, f32[3,256]{1,0:T(4,128)S(1)}, f32[3,256]{1,0:T(4,128)S(1)}, f32[3,64,256]{2,1,0:T(8,128)S(1)}, bf16[4,2048,3,128]{3,1,0,2:T(8,128)(...) while((s32[]{:T(128)}, f32[3,256]{1,0:T(4,128)S(1)}, f32[3,256]{1,0:T(4,128)S(1)}, ...), condition=%wide.region_3.4_spmd.clone, body=%wide.region_0.3_spmd.clone.sunk | while | flops 415387392 | bytes 27674760 | solution.py:52
  140.5 0.0 copy-start.1
  140.5 2.7 %constant_dynamic-slice_fusion.2 = bf16[1,2048,3,128]{3,1,0,2:T(8,128)(2,1)} fusion(bf16[4,2048,3,128]{3,1,0,2:T(8,128)(2,1)} %get-tuple-element.148, s32[]{:T(128)S(6)} %copy.19), kind=kLoop, calls=%fused_computation.15.clone.1 | loop fusion | bytes 3145732 | tf_op jit(solution)/shard_map/while/body/jit(dynamic_index_in_dim)/dynamic_slice | solution.py:52
  143.2 1.7 copy.13
  145.0 0.0 copy-done.1
  145.0 1.0 bitcast_reduce_fusion.2
  146.0 1.0 fusion.28
  147.1 1.2 fusion.30
  148.3 0.0 copy-start.1
  148.3 2.7 %constant_dynamic-slice_fusion.2 = bf16[1,2048,3,128]{3,1,0,2:T(8,128)(2,1)} fusion(bf16[4,2048,3,128]{3,1,0,2:T(8,128)(2,1)} %get-tuple-element.148, s32[]{:T(128)S(6)} %copy.19), kind=kLoop, calls=%fused_computation.15.clone.1 | loop fusion | bytes 3145732 | tf_op jit(solution)/shard_map/while/body/jit(dynamic_index_in_dim)/dynamic_slice | solution.py:52
  151.0 1.7 copy.13
  152.7 0.0 copy-done.1
  152.7 1.0 bitcast_reduce_fusion.2
  153.8 1.0 fusion.28
  154.8 1.2 fusion.30
  156.0 0.0 copy-start.1
  156.0 2.7 %constant_dynamic-slice_fusion.2 = bf16[1,2048,3,128]{3,1,0,2:T(8,128)(2,1)} fusion(bf16[4,2048,3,128]{3,1,0,2:T(8,128)(2,1)} %get-tuple-element.148, s32[]{:T(128)S(6)} %copy.19), kind=kLoop, calls=%fused_computation.15.clone.1 | loop fusion | bytes 3145732 | tf_op jit(solution)/shard_map/while/body/jit(dynamic_index_in_dim)/dynamic_slice | solution.py:52
  158.7 1.7 copy.13
  160.5 0.0 copy-done.1
  160.5 1.0 bitcast_reduce_fusion.2
  161.5 1.0 fusion.28
  162.6 1.2 fusion.30
  163.8 0.0 copy-start.1
  163.8 2.7 %constant_dynamic-slice_fusion.2 = bf16[1,2048,3,128]{3,1,0,2:T(8,128)(2,1)} fusion(bf16[4,2048,3,128]{3,1,0,2:T(8,128)(2,1)} %get-tuple-element.148, s32[]{:T(128)S(6)} %copy.19), kind=kLoop, calls=%fused_computation.15.clone.1 | loop fusion | bytes 3145732 | tf_op jit(solution)/shard_map/while/body/jit(dynamic_index_in_dim)/dynamic_slice | solution.py:52
  166.5 1.7 copy.13
  168.2 0.0 copy-done.1
  168.2 1.0 bitcast_reduce_fusion.2
  169.3 1.0 fusion.28
  170.3 1.2 fusion.30
  171.5 0.7 divide_convert_fusion
  172.2 0.0 all-gather.5.cloned.1.call-update
  172.2 76.5 %all-gather.5.cloned.1.call-done = bf16[3072,256]{1,0:T(8,128)(2,1)} async-done(((bf16[192,256]{1,0:T(8,128)(2,1)}), bf16[3072,256]{1,0:T(8,128)(2,1)}) %all-gather.5.cloned.1.call-update) | async-done | bytes 1572880 | tf_op jit(solution)/shard_map/all_gather | solution.py:58
  248.7 0.0 copy-done
  248.7 0.0 copy-done.2
  248.7 0.0 copy-done.3
  248.7 2.5 fusion.15
  (15 shorter events, 0.1 us)
Async XLA Ops:
  6.5 242.2 %copy-start = (bf16[192,3072]{1,0:T(8,128)(2,1)S(1)}, bf16[192,3072]{1,0:T(8,128)(2,1)}, u32[]{:S(2)}) copy-start(bf16[192,3072]{1,0:T(8,128)(2,1)} %param.13) | copy-start | bytes 3538948
  6.5 132.4 %all-gather.3.cloned.1.call-start = ((), (), s32[]{:S(2)}) async-start(), calls=%async_computation | async-start | bytes 6488064 | tf_op jit(solution)/shard_map/all_gather | solution.py:41
  7.3 241.4 %all-gather.5.cloned.1.call-start = ((), (), s32[]{:S(2)}) async-start(), calls=%async_computation.1 | async-start | bytes 1671168 | tf_op jit(solution)/shard_map/all_gather | solution.py:58
  140.5 108.2 %copy-start.2 = (bf16[192,256]{1,0:T(8,128)(2,1)S(1)}, bf16[192,256]{1,0:T(8,128)(2,1)}, u32[]{:S(2)}) copy-start(bf16[192,256]{1,0:T(8,128)(2,1)} %param.11) | copy-start | bytes 294916
  140.5 108.2 %copy-start.3 = (f32[192]{0:T(256)S(1)}, f32[192]{0:T(256)}, u32[]{:S(2)}) copy-start(f32[192]{0:T(256)} %param.12) | copy-start | bytes 2308
  140.5 4.4 %copy-start.1 = (bf16[3,64,256]{2,1,0:T(8,128)(2,1)S(1)}, bf16[3,64,256]{2,1,0:T(8,128)(2,1)}, u32[]{:S(2)}) copy-start(bf16[3,64,256]{2,1,0:T(8,128)(2,1)} %get-tuple-element.149) | copy-start | bytes 294916 | tf_op jit(solution)/shard_map/while
  148.3 4.4 %copy-start.1 = (bf16[3,64,256]{2,1,0:T(8,128)(2,1)S(1)}, bf16[3,64,256]{2,1,0:T(8,128)(2,1)}, u32[]{:S(2)}) copy-start(bf16[3,64,256]{2,1,0:T(8,128)(2,1)} %get-tuple-element.149) | copy-start | bytes 294916 | tf_op jit(solution)/shard_map/while
  156.0 4.4 %copy-start.1 = (bf16[3,64,256]{2,1,0:T(8,128)(2,1)S(1)}, bf16[3,64,256]{2,1,0:T(8,128)(2,1)}, u32[]{:S(2)}) copy-start(bf16[3,64,256]{2,1,0:T(8,128)(2,1)} %get-tuple-element.149) | copy-start | bytes 294916 | tf_op jit(solution)/shard_map/while
  163.8 4.4 %copy-start.1 = (bf16[3,64,256]{2,1,0:T(8,128)(2,1)S(1)}, bf16[3,64,256]{2,1,0:T(8,128)(2,1)}, u32[]{:S(2)}) copy-start(bf16[3,64,256]{2,1,0:T(8,128)(2,1)} %get-tuple-element.149) | copy-start | bytes 294916 | tf_op jit(solution)/shard_map/while
Sparse Core Ops, SparseCore 0:
  9.4 129.4 all-gather.2
  172.3 76.3 all-gather.4
where the time goes:
time: 258 us
  waiting for transfers between devices  209 us (81%)
  local copies, waits for them, and re-layouts  19.3 us (7%)
  between operations  13.4 us (5%)
  matrix products  11.3 us (4%)
  other arithmetic  4.91 us (2%)
    all_gather x1, waiting for transfers between devices, on_device(): gathered = lax.all_gather(stale_kv, 'patch', axis=0, tiled=True)  132 us
    all_gather x1, waiting for transfers between devices, on_device(): all_heads = lax.all_gather(attended, 'head', axis=0, tiled=True)  76.5 us
    dynamic_slice x8, local copies, waits for them, and re-layouts, on_device(): result, unused = lax.scan(step_fn, initial, (indices, stacked))  17.6 us
  transfers between devices with their start and end apart: 2, of which 2 were waited for; matrix products, arithmetic and copies ran while one was open for 0% of the time, Pallas kernels for 0%

commit v1 on v0

v1 whole, which is shorter than its diff:
```python
import functools
import math

import jax
import jax.numpy as jnp
from jax import lax
from jax.experimental import pallas as pl
from jax.experimental.pallas import tpu as pltpu
from jax.sharding import PartitionSpec as P

MESH = pl.DeviceIdType.MESH
HEADS = 3
HD = 64
TOK = 256
RING = 16
LOG2E = 1.4426950408889634
HALF = TOK // 2
ROWS = HD + 16


def fused(q_in, fresh_in, stale_in, w_in, out, kv, fresh, qb, qx, wb, wp, qs, acc, top,
          opart, ostat, oin, ostat_in, att, load_sem, z_send, z_recv, y_send, y_recv,
          g_send, g_recv, c_send, c_recv):
    patch = lax.axis_index("patch")
    head = lax.axis_index("head")
    y_lo, z = patch // RING, patch % RING
    y_hi, x, core = head // 8, (head // 2) % 4, head % 2
    right = (y_lo * RING + (z + 1) % RING, head)
    left = (y_lo * RING + (z + RING - 1) % RING, head)
    across = ((1 - y_lo) * RING + z, head)
    sibling = (patch, head + 1 - 2 * core)

    def plane(j):
        return (patch, ((y_hi + j // 4) % 2) * 8 + ((x + j % 4) % 4) * 2 + core)

    def plane_back(j):
        return ((y_hi + j // 4) % 2) * 8 + ((x + 4 - j % 4) % 4) * 2 + core

    loads = [
        pltpu.make_async_copy(stale_in, kv.at[:, 0], load_sem.at[0]),
        pltpu.make_async_copy(q_in, qb, load_sem.at[1]),
        pltpu.make_async_copy(fresh_in, fresh, load_sem.at[2]),
        pltpu.make_async_copy(w_in, wb, load_sem.at[3]),
    ]
    for load in loads:
        load.start()

    barrier = pltpu.get_barrier_semaphore()
    partners = [right, left, across, sibling] + [plane(j) for j in range(1, 8)]
    for partner in partners:
        pl.semaphore_signal(barrier, inc=1, device_id=partner, device_id_type=MESH)
    pl.semaphore_wait(barrier, len(partners))

    def remote(src, dst, send, recv, device):
        return pltpu.make_async_remote_copy(
            src_ref=src, dst_ref=dst, send_sem=send, recv_sem=recv,
            device_id=device, device_id_type=MESH)

    def hop_right(h, s, rows=slice(None)):
        return remote(kv.at[h, s, rows], kv.at[h, s + 1, rows], z_send.at[0, h, s],
                      z_recv.at[0, h, s], right)

    def hop_left(h, s, rows=slice(None)):
        return remote(kv.at[h, (RING - s) % RING, rows], kv.at[h, RING - 1 - s, rows],
                      z_send.at[1, h, s], z_recv.at[1, h, s], left)

    low, high = pl.ds(0, HALF), pl.ds(HALF, HALF)

    loads[0].wait()
    for h in range(HEADS):
        hop_right(h, 0).start()
        hop_left(h, 0).start()
    loads[1].wait()
    q_move = remote(qb, qx, y_send.at[0], y_recv.at[0], across)
    q_move.start()

    lane = lax.broadcasted_iota(jnp.int32, (1, 2 * HD), 1)

    def with_ones(block):
        swapped = jnp.where(lane < HD, jnp.ones_like(block), block)
        return swapped.T[HD - 16:]

    def first(h, block, lo):
        cols = pl.ds(lo, TOK)
        scores = jnp.dot(block, qs[h, :, cols], preferred_element_type=jnp.float32)
        high_score = jnp.max(scores, axis=0, keepdims=True)
        weights = jnp.exp2((scores - high_score) * LOG2E).astype(jnp.bfloat16)
        acc[h, :, cols] = jnp.dot(with_ones(block), weights, preferred_element_type=jnp.float32)
        top[h, :, cols] = high_score

    def update(h, block, lo, width):
        cols = pl.ds(lo, width)
        scores = jnp.dot(block, qs[h, :, cols], preferred_element_type=jnp.float32)
        old = top[h, :, cols]
        new = jnp.maximum(old, jnp.max(scores, axis=0, keepdims=True))
        weights = jnp.exp2((scores - new) * LOG2E).astype(jnp.bfloat16)
        part = jnp.dot(with_ones(block), weights, preferred_element_type=jnp.float32)
        acc[h, :, cols] = acc[h, :, cols] * jnp.exp2((old - new) * LOG2E) + part
        top[h, :, cols] = new

    def place_queries(src, lo):
        for h in range(HEADS):
            scaled = src[pl.ds(h * HD, HD), :] * jnp.bfloat16(1.0 / math.sqrt(HD))
            qs[h, pl.ds(0, HD), pl.ds(lo, TOK)] = scaled
            qs[h, pl.ds(HD, HD), pl.ds(lo, TOK)] = jnp.zeros((HD, TOK), jnp.bfloat16)

    place_queries(qb, 0)
    loads[2].wait()

    def own_fresh(h, carry):
        first(h, fresh[h], 0)
        return carry

    lax.fori_loop(0, HEADS, own_fresh, 0)

    loads[3].wait()
    for h in range(HEADS):
        for k in range(8):
            pair = [wb[:, pl.ds((2 * k + e) * HEADS * HD + h * HD, HD)] for e in range(2)]
            wp[h, :, pl.ds(k * 128, 128)] = jnp.concatenate(pair, axis=1)

    q_move.wait_recv()
    place_queries(qx, TOK)

    def own_stale(h, carry):
        first(h, kv[h, 0], TOK)
        return carry

    lax.fori_loop(0, HEADS, own_stale, 0)

    def ring_step(t, carry):
        s, h = 1 + t // HEADS, t % HEADS
        hop_right(h, s - 1).wait_recv()

        @pl.when(s < 7)
        def _():
            hop_right(h, s).start()

        @pl.when(s == 7)
        def _():
            hop_right(h, s, low).start()

        hop_left(h, s - 1).wait_recv()

        @pl.when(s < 7)
        def _():
            hop_left(h, s).start()

        @pl.when(s == 7)
        def _():
            hop_left(h, s, high).start()

        update(h, kv[h, s], 0, 2 * TOK)
        update(h, kv[h, RING - s], 0, 2 * TOK)
        return carry

    lax.fori_loop(0, 7 * HEADS, ring_step, 0)

    def o_moves(h):
        return (remote(opart.at[h], oin.at[h], y_send.at[1 + h], y_recv.at[1 + h], across),
                remote(ostat.at[h], ostat_in.at[h], y_send.at[4 + h], y_recv.at[4 + h], across))

    def last_step(h, carry):
        hop_right(h, 7, low).wait_recv()
        hop_left(h, 7, high).wait_recv()
        block = kv[h, 8]
        update(h, block, TOK, TOK)
        cols = pl.ds(TOK, TOK)
        total = acc[h, pl.ds(0, 8), cols][0:1]
        opart[h] = (acc[h, pl.ds(16, HD), cols] / total).astype(jnp.bfloat16)
        ostat[h, pl.ds(0, 1)] = top[h, :, cols]
        ostat[h, pl.ds(1, 1)] = total
        for move in o_moves(h):
            move.start()
        update(h, block, 0, TOK)
        return carry

    ostat[...] = jnp.zeros_like(ostat)
    lax.fori_loop(0, HEADS, last_step, 0)

    def sent(t, carry):
        s, h = t // HEADS, t % HEADS
        hop_right(h, s).wait_send()
        hop_left(h, s).wait_send()
        return carry

    lax.fori_loop(0, 7 * HEADS, sent, 0)
    for h in range(HEADS):
        hop_right(h, 7, low).wait_send()
        hop_left(h, 7, high).wait_send()
    q_move.wait_send()

    def g_move(h, j):
        return remote(att.at[h, head], att.at[h, head], g_send.at[h, j], g_recv.at[h, j], plane(j))

    def c_move(h, j):
        slot = plane_back(j)
        return remote(att.at[h, slot], att.at[h, slot], c_send.at[h, j], c_recv.at[h, j], sibling)

    def combine(h, carry):
        for move in o_moves(h):
            move.wait_recv()
        cols = pl.ds(0, TOK)
        top_a, top_b = top[h, :, cols], ostat_in[h, pl.ds(0, 1)]
        new = jnp.maximum(top_a, top_b)
        scale_a = jnp.exp2((top_a - new) * LOG2E)
        total_a = acc[h, pl.ds(0, 8), cols][0:1] * scale_a
        total_b = ostat_in[h, pl.ds(1, 1)] * jnp.exp2((top_b - new) * LOG2E)
        inverse = 1.0 / (total_a + total_b)
        mixed = (acc[h, pl.ds(16, HD), cols] * (scale_a * inverse)
                 + oin[h].astype(jnp.float32) * (total_b * inverse))
        att[h, head] = mixed.astype(jnp.bfloat16)
        for j in (6, 5, 7, 4, 2, 1, 3):
            g_move(h, j).start()
        c_move(h, 0).start()
        return carry

    lax.fori_loop(0, HEADS, combine, 0)

    def project(h, carry):
        for j in (1, 3, 2, 4, 5, 7, 6):
            g_move(h, j).wait_recv()
            c_move(h, j).start()
        for j in range(8):
            c_move(h, j).wait_recv()
        part = jnp.dot(wp[h], att[h].reshape(16 * HD, TOK), preferred_element_type=jnp.float32)
        out[...] = out[...] + part
        return carry

    out[...] = jnp.zeros_like(out)
    lax.fori_loop(0, HEADS, project, 0)

    def drain(h, carry):
        for move in o_moves(h):
            move.wait_send()
        for j in range(1, 8):
            g_move(h, j).wait_send()
        for j in range(8):
            c_move(h, j).wait_send()
        return carry

    lax.fori_loop(0, HEADS, drain, 0)


def on_device(queries, fresh_kv, stale_kv, residual, gate, w_out):
    bf16, f32 = jnp.bfloat16, jnp.float32
    any_space = pl.BlockSpec(memory_space=pl.ANY)
    dma = pltpu.SemaphoreType.DMA
    projected = pl.pallas_call(
        fused,
        out_shape=jax.ShapeDtypeStruct((HEADS * HD, TOK), f32),
        in_specs=[any_space] * 4,
        out_specs=pl.BlockSpec(memory_space=pltpu.VMEM),
        scratch_shapes=[
            pltpu.VMEM((HEADS, RING, TOK, 2 * HD), bf16),
            pltpu.VMEM((HEADS, TOK, 2 * HD), bf16),
            pltpu.VMEM((HEADS * HD, TOK), bf16),
            pltpu.VMEM((HEADS * HD, TOK), bf16),
            pltpu.VMEM((HEADS * HD, 16 * HEADS * HD), bf16),
            pltpu.VMEM((HEADS, HEADS * HD, 16 * HD), bf16),
            pltpu.VMEM((HEADS, 2 * HD, 2 * TOK), bf16),
            pltpu.VMEM((HEADS, ROWS, 2 * TOK), f32),
            pltpu.VMEM((HEADS, 1, 2 * TOK), f32),
            pltpu.VMEM((HEADS, HD, TOK), bf16),
            pltpu.VMEM((HEADS, 8, TOK), f32),
            pltpu.VMEM((HEADS, HD, TOK), bf16),
            pltpu.VMEM((HEADS, 8, TOK), f32),
            pltpu.VMEM((HEADS, 16, HD, TOK), bf16),
            dma((4,)),
            dma((2, HEADS, 8)),
            dma((2, HEADS, 8)),
            dma((7,)),
            dma((7,)),
            dma((HEADS, 8)),
            dma((HEADS, 8)),
            dma((HEADS, 8)),
            dma((HEADS, 8)),
        ],
        compiler_params=pltpu.CompilerParams(
            collective_id=0, has_side_effects=True, vmem_limit_bytes=40 * 1024 * 1024),
        cost_estimate=pl.CostEstimate(
            flops=2_000_000_000, bytes_accessed=4_000_000, transcendentals=6_500_000),
    )(queries, fresh_kv.transpose(1, 0, 2), stale_kv.transpose(1, 0, 2), w_out)
    result = residual.astype(f32) + gate[:, None] * projected
    return result.astype(bf16)


def solution(mesh):
    placed = (
        P("head", "patch"),
        P("patch", "head", None),
        P("patch", "head", None),
        P("head", "patch"),
        P("head"),
        P("head", None),
    )
    return jax.shard_map(
        on_device, mesh=mesh, in_specs=placed, out_specs=P("head", "patch"), check_vma=False
    )
```

time: 258 us -> 71.8 us (0.28)
  waiting for transfers between devices: 209 us -> 0 us
  Pallas kernels: 0 us -> 66.8 us
  local copies, waits for them, and re-layouts: 19.3 us -> 4.02 us
  between operations: 13.4 us -> 0.03 us
  matrix products: 11.3 us -> 0 us
  other arithmetic: 4.91 us -> 0.74 us
    all_gather x2 -> x0, waiting for transfers between devices: 208 us -> none  [the longest x1 132 us: on_device(): gathered = lax.all_gather(stale_kv, 'patch', axis=0, tiled=True)]
    pallas_call x0 -> x1, Pallas kernels: none -> 66.8 us  [on_device(): pl.pallas_call(fused, out_shape=jax.ShapeDtypeStruct((HEADS * HD, TOK), f...]
    dynamic_slice x8 -> x0, local copies, waits for them, and re-layouts: 17.6 us -> none  [on_device(): result, unused = lax.scan(step_fn, initial, (indices, stacked))]
    dot_general x9 -> x0, matrix products: 11.3 us -> none  [the longest x4 4.61 us: attend(): jnp.einsum('hij,jhd->hdi', probs, value_part, preferred_element_type=jnp....]
    reduce_sum x4 -> x0, other arithmetic: 4.14 us -> none  [attend(): total_now = total_now * rescale + jnp.sum(weights_exp, axis=2)]
    unnamed x6 -> x12, local copies, waits for them, and re-layouts: 0.01 us -> 4.02 us
  transfers between devices with their start and end apart: 2 -> 0, of which waited for: 2 -> 0; matrix products, arithmetic and copies ran while one was open for 0% -> 0% of each run, Pallas kernels for 0% -> 0%
where the time goes in v1:
time: 71.8 us; the launch traced here: 71.6 us
  Pallas kernels  66.8 us (93%)
  local copies, waits for them, and re-layouts  4.02 us (6%)
  other arithmetic  0.74 us (1%)
    pallas_call x1, Pallas kernels, on_device(): pl.pallas_call(fused, out_shape=jax.ShapeDtypeStruct((HEADS * HD, TOK), f...  66.8 us
    unnamed x12, local copies, waits for them, and re-layouts  4.02 us

profile of v1, /device:TPU:1, one launch (start us, length us, event | category | flops | bytes accessed | tf_op | source)
XLA Modules:
  0.0 71.6 jit_solution(4062564557532108026)
XLA Ops:
  0.0 0.0 copy-start
  0.0 1.3 %copy-done = bf16[192,3072]{1,0:T(8,128)(2,1)S(1)} copy-done((bf16[192,3072]{1,0:T(8,128)(2,1)S(1)}, bf16[192,3072]{1,0:T(8,128)(2,1)}, u32[]{:S(2)}) %copy-start) | copy-done | bytes 1179672
  1.3 0.0 copy-start.1
  1.3 0.9 %copy-done.1 = bf16[256,3,128]{2,0,1:T(8,128)(2,1)S(1)} copy-done((bf16[256,3,128]{2,0,1:T(8,128)(2,1)S(1)}, bf16[256,3,128]{2,0,1:T(8,128)(2,1)}, u32[]{:S(2)}) %copy-start.1) | copy-done | bytes 196632
  2.2 0.0 copy-start.2
  2.2 0.9 %copy-done.2 = bf16[256,3,128]{2,0,1:T(8,128)(2,1)S(1)} copy-done((bf16[256,3,128]{2,0,1:T(8,128)(2,1)S(1)}, bf16[256,3,128]{2,0,1:T(8,128)(2,1)}, u32[]{:S(2)}) %copy-start.2) | copy-done | bytes 196632
  3.1 0.0 copy-start.3
  3.1 0.9 %copy-done.3 = bf16[192,256]{1,0:T(8,128)(2,1)S(1)} copy-done((bf16[192,256]{1,0:T(8,128)(2,1)S(1)}, bf16[192,256]{1,0:T(8,128)(2,1)}, u32[]{:S(2)}) %copy-start.3) | copy-done | bytes 98328
  4.0 0.0 copy-start.4
  4.0 0.0 copy-start.5
  4.0 66.8 %shard_map.64 = f32[192,256]{1,0:T(8,128)S(1)} custom-call(bf16[192,256]{1,0:T(8,128)(2,1)S(1)} %copy-done.3, bf16[3,256,128]{2,1,0:T(8,128)(2,1)S(1)} %bitcast.2, bf16[3,256,128]{2,1,0:T(8,128)(2,1)S(1)} %bitcast.3, bf16[192,3072]{1,0:T(8,128)(2,1)S(1)} %copy-done), custom_call_target="tpu_custom_call" | custom-call | flops 2000000000 | bytes 4000000 | tf_op jit(solution)/shard_map/pallas_call | solution.py:249
  70.8 0.0 copy-done.4
  70.8 0.0 copy-done.5
  70.8 0.7 %add_convert_fusion = bf16[192,256]{1,0:T(8,128)(2,1)} fusion(f32[192,256]{1,0:T(8,128)S(1)} %shard_map.64, bf16[192,256]{1,0:T(8,128)(2,1)S(1)} %copy-done.4, f32[192]{0:T(256)S(1)} %copy-done.5), kind=kLoop, calls=%fused_computation | loop fusion | flops 196608 | bytes 393984 | tf_op jit(solution)/shard_map/convert_element_type | solution.py:285
Async XLA Ops:
  0.0 1.3 %copy-start = (bf16[192,3072]{1,0:T(8,128)(2,1)S(1)}, bf16[192,3072]{1,0:T(8,128)(2,1)}, u32[]{:S(2)}) copy-start(bf16[192,3072]{1,0:T(8,128)(2,1)} %w_in.1) | copy-start | bytes 3538948
  1.3 0.9 %copy-start.1 = (bf16[256,3,128]{2,0,1:T(8,128)(2,1)S(1)}, bf16[256,3,128]{2,0,1:T(8,128)(2,1)}, u32[]{:S(2)}) copy-start(bf16[256,3,128]{2,0,1:T(8,128)(2,1)} %param.7) | copy-start | bytes 589828
  2.2 0.9 %copy-start.2 = (bf16[256,3,128]{2,0,1:T(8,128)(2,1)S(1)}, bf16[256,3,128]{2,0,1:T(8,128)(2,1)}, u32[]{:S(2)}) copy-start(bf16[256,3,128]{2,0,1:T(8,128)(2,1)} %param.8) | copy-start | bytes 589828
  3.1 0.9 %copy-start.3 = (bf16[192,256]{1,0:T(8,128)(2,1)S(1)}, bf16[192,256]{1,0:T(8,128)(2,1)}, u32[]{:S(2)}) copy-start(bf16[192,256]{1,0:T(8,128)(2,1)} %q_in.1) | copy-start | bytes 294916
  4.0 66.8 %copy-start.4 = (bf16[192,256]{1,0:T(8,128)(2,1)S(1)}, bf16[192,256]{1,0:T(8,128)(2,1)}, u32[]{:S(2)}) copy-start(bf16[192,256]{1,0:T(8,128)(2,1)} %param.9) | copy-start | bytes 294916
  4.0 66.8 %copy-start.5 = (f32[192]{0:T(256)S(1)}, f32[192]{0:T(256)}, u32[]{:S(2)}) copy-start(f32[192]{0:T(256)} %param.10) | copy-start | bytes 2308

commit v2 on v1

--- a/solution.py
+++ b/solution.py
@@ -15,6 +15,7 @@
 RING = 16
 LOG2E = 1.4426950408889634
 HALF = TOK // 2
+RIGHT_HOPS, LEFT_HOPS = 7, 8
 ROWS = HD + 16
 
 
@@ -56,20 +57,21 @@
             src_ref=src, dst_ref=dst, send_sem=send, recv_sem=recv,
             device_id=device, device_id_type=MESH)
 
-    def hop_right(h, s, rows=slice(None)):
-        return remote(kv.at[h, s, rows], kv.at[h, s + 1, rows], z_send.at[0, h, s],
-                      z_recv.at[0, h, s], right)
-
-    def hop_left(h, s, rows=slice(None)):
+    def hop_right(h, part, s):
+        rows = pl.ds(part * HALF, HALF)
+        return remote(kv.at[h, s, rows], kv.at[h, s + 1, rows], z_send.at[0, h, part, s],
+                      z_recv.at[0, h, part, s], right)
+
+    def hop_left(h, part, s):
+        rows = pl.ds(part * HALF, HALF)
         return remote(kv.at[h, (RING - s) % RING, rows], kv.at[h, RING - 1 - s, rows],
-                      z_send.at[1, h, s], z_recv.at[1, h, s], left)
-
-    low, high = pl.ds(0, HALF), pl.ds(HALF, HALF)
+                      z_send.at[1, h, part, s], z_recv.at[1, h, part, s], left)
 
     loads[0].wait()
     for h in range(HEADS):
-        hop_right(h, 0).start()
-        hop_left(h, 0).start()
+        for part in range(2):
+            hop_right(h, part, 0).start()
+            hop_left(h, part, 0).start()
     loads[1].wait()
     q_move = remote(qb, qx, y_send.at[0], y_recv.at[0], across)
     q_move.start()
@@ -129,41 +131,29 @@
     lax.fori_loop(0, HEADS, own_stale, 0)
 
     def ring_step(t, carry):
-        s, h = 1 + t // HEADS, t % HEADS
-        hop_right(h, s - 1).wait_recv()
-
-        @pl.when(s < 7)
+        s, h, part = 1 + t // (2 * HEADS), (t // 2) % HEADS, t % 2
+        hop_right(h, part, s - 1).wait_recv()
+
+        @pl.when(s < RIGHT_HOPS)
         def _():
-            hop_right(h, s).start()
-
-        @pl.when(s == 7)
-        def _():
-            hop_right(h, s, low).start()
-
-        hop_left(h, s - 1).wait_recv()
-
-        @pl.when(s < 7)
-        def _():
-            hop_left(h, s).start()
-
-        @pl.when(s == 7)
-        def _():
-            hop_left(h, s, high).start()
-
-        update(h, kv[h, s], 0, 2 * TOK)
-        update(h, kv[h, RING - s], 0, 2 * TOK)
-        return carry
-
-    lax.fori_loop(0, 7 * HEADS, ring_step, 0)
+            hop_right(h, part, s).start()
+
+        hop_left(h, part, s - 1).wait_recv()
+        hop_left(h, part, s).start()
+        rows = pl.ds(part * HALF, HALF)
+        update(h, jnp.concatenate([kv[h, s, rows], kv[h, RING - s, rows]], axis=0), 0, 2 * TOK)
+        return carry
+
+    lax.fori_loop(0, RIGHT_HOPS * HEADS * 2, ring_step, 0)
 
     def o_moves(h):
         return (remote(opart.at[h], oin.at[h], y_send.at[1 + h], y_recv.at[1 + h], across),
                 remote(ostat.at[h], ostat_in.at[h], y_send.at[4 + h], y_recv.at[4 + h], across))
 
     def last_step(h, carry):
-        hop_right(h, 7, low).wait_recv()
-        hop_left(h, 7, high).wait_recv()
-        block = kv[h, 8]
+        for part in range(2):
+            hop_left(h, part, LEFT_HOPS - 1).wait_recv()
+        block = kv[h, RING - LEFT_HOPS]
         update(h, block, TOK, TOK)
         cols = pl.ds(TOK, TOK)
         total = acc[h, pl.ds(0, 8), cols][0:1]
@@ -180,14 +170,16 @@
 
     def sent(t, carry):
         s, h = t // HEADS, t % HEADS
-        hop_right(h, s).wait_send()
-        hop_left(h, s).wait_send()
-        return carry
-
-    lax.fori_loop(0, 7 * HEADS, sent, 0)
-    for h in range(HEADS):
-        hop_right(h, 7, low).wait_send()
-        hop_left(h, 7, high).wait_send()
+        for part in range(2):
+            hop_left(h, part, s).wait_send()
+
+            @pl.when(s < RIGHT_HOPS)
+            def _():
+                hop_right(h, part, s).wait_send()
+
+        return carry
+
+    lax.fori_loop(0, LEFT_HOPS * HEADS, sent, 0)
     q_move.wait_send()
 
     def g_move(h, j):
@@ -217,7 +209,19 @@
 
     lax.fori_loop(0, HEADS, combine, 0)
 
+    def drain(h):
+        for move in o_moves(h):
+            move.wait_send()
+        for j in range(1, 8):
+            g_move(h, j).wait_send()
+        for j in range(8):
+            c_move(h, j).wait_send()
+
     def project(h, carry):
+        @pl.when(h > 0)
+        def _():
+            drain(h - 1)
+
         for j in (1, 3, 2, 4, 5, 7, 6):
             g_move(h, j).wait_recv()
             c_move(h, j).start()
@@ -229,27 +233,18 @@
 
     out[...] = jnp.zeros_like(out)
     lax.fori_loop(0, HEADS, project, 0)
-
-    def drain(h, carry):
-        for move in o_moves(h):
-            move.wait_send()
-        for j in range(1, 8):
-            g_move(h, j).wait_send()
-        for j in range(8):
-            c_move(h, j).wait_send()
-        return carry
-
-    lax.fori_loop(0, HEADS, drain, 0)
+    drain(HEADS - 1)
 
 
 def on_device(queries, fresh_kv, stale_kv, residual, gate, w_out):
     bf16, f32 = jnp.bfloat16, jnp.float32
-    any_space = pl.BlockSpec(memory_space=pl.ANY)
+    in_hbm = pl.BlockSpec(memory_space=pltpu.HBM)
     dma = pltpu.SemaphoreType.DMA
+    operands = (queries, fresh_kv.transpose(1, 0, 2), stale_kv.transpose(1, 0, 2), w_out)
     projected = pl.pallas_call(
         fused,
         out_shape=jax.ShapeDtypeStruct((HEADS * HD, TOK), f32),
-        in_specs=[any_space] * 4,
+        in_specs=[in_hbm] * 4,
         out_specs=pl.BlockSpec(memory_space=pltpu.VMEM),
         scratch_shapes=[
             pltpu.VMEM((HEADS, RING, TOK, 2 * HD), bf16),
@@ -267,8 +262,8 @@
             pltpu.VMEM((HEADS, 8, TOK), f32),
             pltpu.VMEM((HEADS, 16, HD, TOK), bf16),
             dma((4,)),
-            dma((2, HEADS, 8)),
-            dma((2, HEADS, 8)),
+            dma((2, HEADS, 2, LEFT_HOPS)),
+            dma((2, HEADS, 2, LEFT_HOPS)),
             dma((7,)),
             dma((7,)),
             dma((HEADS, 8)),
@@ -280,7 +275,7 @@
             collective_id=0, has_side_effects=True, vmem_limit_bytes=40 * 1024 * 1024),
         cost_estimate=pl.CostEstimate(
             flops=2_000_000_000, bytes_accessed=4_000_000, transcendentals=6_500_000),
-    )(queries, fresh_kv.transpose(1, 0, 2), stale_kv.transpose(1, 0, 2), w_out)
+    )(*[pltpu.with_memory_space_constraint(operand, pltpu.HBM) for operand in operands])
     result = residual.astype(f32) + gate[:, None] * projected
     return result.astype(bf16)
 

time: 71.8 us -> 68.4 us (0.953)
  local copies, waits for them, and re-layouts: 4.02 us -> 0.01 us
    unnamed x12 -> x4, local copies, waits for them, and re-layouts: 4.02 us -> 0.01 us
where the time goes in v2:
time: 68.4 us; the launch traced here: 68.3 us
  Pallas kernels  67.5 us (99%)
  other arithmetic  0.74 us (1%)
    pallas_call x1, Pallas kernels, on_device(): pl.pallas_call(fused, out_shape=jax.ShapeDtypeStruct((HEADS * HD, TOK), f...  67.5 us

profile of v2, /device:TPU:1, one launch (start us, length us, event | category | flops | bytes accessed | tf_op | source)
XLA Modules:
  0.0 68.3 jit_solution(6684887145511333726)
XLA Ops:
  0.0 0.0 copy-start
  0.0 0.0 copy-start.1
  0.0 67.5 %shard_map.64 = f32[192,256]{1,0:T(8,128)S(1)} custom-call(bf16[192,256]{1,0:T(8,128)(2,1)} %q_in.1, bf16[3,256,128]{2,1,0:T(8,128)(2,1)} %bitcast.2, bf16[3,256,128]{2,1,0:T(8,128)(2,1)} %bitcast.3, bf16[192,3072]{1,0:T(8,128)(2,1)} %w_in.1), custom_call_target="tpu_custom_call" | custom-call | flops 2000000000 | bytes 4000000 | tf_op jit(solution)/shard_map/pallas_call | solution.py:244
  67.5 0.0 copy-done
  67.5 0.0 copy-done.1
  67.5 0.7 %add_convert_fusion = bf16[192,256]{1,0:T(8,128)(2,1)} fusion(f32[192,256]{1,0:T(8,128)S(1)} %shard_map.64, bf16[192,256]{1,0:T(8,128)(2,1)S(1)} %copy-done, f32[192]{0:T(256)S(1)} %copy-done.1), kind=kLoop, calls=%fused_computation | loop fusion | flops 196608 | bytes 393984 | tf_op jit(solution)/shard_map/convert_element_type | solution.py:280
Async XLA Ops:
  0.0 67.5 %copy-start = (bf16[192,256]{1,0:T(8,128)(2,1)S(1)}, bf16[192,256]{1,0:T(8,128)(2,1)}, u32[]{:S(2)}) copy-start(bf16[192,256]{1,0:T(8,128)(2,1)} %param.9) | copy-start | bytes 294916
  0.0 67.5 %copy-start.1 = (f32[192]{0:T(256)S(1)}, f32[192]{0:T(256)}, u32[]{:S(2)}) copy-start(f32[192]{0:T(256)} %param.10) | copy-start | bytes 2308

commit v3 on v2

--- a/solution.py
+++ b/solution.py
@@ -121,38 +121,90 @@
             pair = [wb[:, pl.ds((2 * k + e) * HEADS * HD + h * HD, HD)] for e in range(2)]
             wp[h, :, pl.ds(k * 128, 128)] = jnp.concatenate(pair, axis=1)
 
+    lead = (1 - (z + 9) // RING) * (2 * HEADS - z)
+
+    def piece(u):
+        return 1 + u // (2 * HEADS), (u // 2) % HEADS, u % 2
+
+    def land_right(t):
+        u = t - lead
+        s, h, part = piece(u)
+
+        @pl.when((u >= 0) & (u < RIGHT_HOPS * 2 * HEADS))
+        def _():
+            hop_right(h, part, s - 1).wait_recv()
+
+            @pl.when(s < RIGHT_HOPS)
+            def _():
+                hop_right(h, part, s).start()
+
+    def land_left(t):
+        s, h, part = piece(t)
+        hop_left(h, part, s - 1).wait_recv()
+
+        @pl.when(s < LEFT_HOPS)
+        def _():
+            hop_left(h, part, s).start()
+
+    def attend_right(t):
+        u = t - lead
+        s, h, part = piece(u)
+
+        @pl.when((u >= 0) & (u < RIGHT_HOPS * 2 * HEADS) & (part == 1))
+        def _():
+            update(h, kv[h, s], 0, 2 * TOK)
+
+    def attend_left(t):
+        s, h, part = piece(t)
+
+        @pl.when(part == 1)
+        def _():
+            update(h, kv[h, RING - s], 0, 2 * TOK)
+
+    def pass_on(t, carry):
+        land_right(t)
+        land_left(t)
+        return carry
+
+    lax.fori_loop(0, HEADS, pass_on, 0)
     q_move.wait_recv()
     place_queries(qx, TOK)
 
     def own_stale(h, carry):
+        pass_on(HEADS + h, 0)
         first(h, kv[h, 0], TOK)
         return carry
 
     lax.fori_loop(0, HEADS, own_stale, 0)
 
     def ring_step(t, carry):
-        s, h, part = 1 + t // (2 * HEADS), (t // 2) % HEADS, t % 2
-        hop_right(h, part, s - 1).wait_recv()
-
-        @pl.when(s < RIGHT_HOPS)
-        def _():
-            hop_right(h, part, s).start()
-
-        hop_left(h, part, s - 1).wait_recv()
-        hop_left(h, part, s).start()
-        rows = pl.ds(part * HALF, HALF)
-        update(h, jnp.concatenate([kv[h, s, rows], kv[h, RING - s, rows]], axis=0), 0, 2 * TOK)
-        return carry
-
-    lax.fori_loop(0, RIGHT_HOPS * HEADS * 2, ring_step, 0)
+        land_right(t)
+        land_left(t)
+        attend_right(t)
+        attend_left(t)
+        late = t // 4 - 1
+        h, side = late // 2, late % 2
+
+        @pl.when((t % 4 == 2) & (late < 2 * HEADS) & ((side == 0) | (2 * h + 1 + lead < 2 * HEADS)))
+        def _():
+            update(h, kv[h, 15 - 14 * side], 0, 2 * TOK)
+
+        return carry
+
+    lax.fori_loop(2 * HEADS, (LEFT_HOPS - 1) * 2 * HEADS, ring_step, 0)
 
     def o_moves(h):
         return (remote(opart.at[h], oin.at[h], y_send.at[1 + h], y_recv.at[1 + h], across),
                 remote(ostat.at[h], ostat_in.at[h], y_send.at[4 + h], y_recv.at[4 + h], across))
 
     def last_step(h, carry):
-        for part in range(2):
-            hop_left(h, part, LEFT_HOPS - 1).wait_recv()
+        def arrive(part, inner):
+            t = (LEFT_HOPS - 1) * 2 * HEADS + 2 * h + part
+            pass_on(t, 0)
+            attend_right(t)
+            return inner
+
+        lax.fori_loop(0, 2, arrive, 0)
         block = kv[h, RING - LEFT_HOPS]
         update(h, block, TOK, TOK)
         cols = pl.ds(TOK, TOK)
@@ -202,7 +254,7 @@
         mixed = (acc[h, pl.ds(16, HD), cols] * (scale_a * inverse)
                  + oin[h].astype(jnp.float32) * (total_b * inverse))
         att[h, head] = mixed.astype(jnp.bfloat16)
-        for j in (6, 5, 7, 4, 2, 1, 3):
+        for j in (1, 3, 4, 2, 5, 7, 6):
             g_move(h, j).start()
         c_move(h, 0).start()
         return carry
@@ -222,7 +274,7 @@
         def _():
             drain(h - 1)
 
-        for j in (1, 3, 2, 4, 5, 7, 6):
+        for j in (1, 3, 4, 2, 5, 7, 6):
             g_move(h, j).wait_recv()
             c_move(h, j).start()
         for j in range(8):

time: 68.4 us -> 64.5 us (0.943)
  Pallas kernels: 67.5 us -> 63.5 us
    pallas_call x1, Pallas kernels: 67.5 us -> 63.5 us  [on_device(): pl.pallas_call(fused, out_shape=jax.ShapeDtypeStruct((HEADS * HD, TOK), f...]
where the time goes in v3:
time: 64.5 us; the launch traced here: 64.3 us
  Pallas kernels  63.5 us (98%)
  other arithmetic  0.74 us (1%)
    pallas_call x1, Pallas kernels, on_device(): pl.pallas_call(fused, out_shape=jax.ShapeDtypeStruct((HEADS * HD, TOK), f...  63.5 us

profile of v3, /device:TPU:1, one launch (start us, length us, event | category | flops | bytes accessed | tf_op | source)
XLA Modules:
  0.0 64.3 jit_solution(7915148962398139839)
XLA Ops:
  0.0 0.0 copy-start
  0.0 0.0 copy-start.1
  0.0 63.5 %shard_map.64 = f32[192,256]{1,0:T(8,128)S(1)} custom-call(bf16[192,256]{1,0:T(8,128)(2,1)} %q_in.1, bf16[3,256,128]{2,1,0:T(8,128)(2,1)} %bitcast.2, bf16[3,256,128]{2,1,0:T(8,128)(2,1)} %bitcast.3, bf16[192,3072]{1,0:T(8,128)(2,1)} %w_in.1), custom_call_target="tpu_custom_call" | custom-call | flops 2000000000 | bytes 4000000 | tf_op jit(solution)/shard_map/pallas_call | solution.py:296
  63.5 0.0 copy-done
  63.5 0.0 copy-done.1
  63.5 0.7 %add_convert_fusion = bf16[192,256]{1,0:T(8,128)(2,1)} fusion(f32[192,256]{1,0:T(8,128)S(1)} %shard_map.64, bf16[192,256]{1,0:T(8,128)(2,1)S(1)} %copy-done, f32[192]{0:T(256)S(1)} %copy-done.1), kind=kLoop, calls=%fused_computation | loop fusion | flops 196608 | bytes 393984 | tf_op jit(solution)/shard_map/convert_element_type | solution.py:332
Async XLA Ops:
  0.0 63.5 %copy-start = (bf16[192,256]{1,0:T(8,128)(2,1)S(1)}, bf16[192,256]{1,0:T(8,128)(2,1)}, u32[]{:S(2)}) copy-start(bf16[192,256]{1,0:T(8,128)(2,1)} %param.9) | copy-start | bytes 294916
  0.0 63.5 %copy-start.1 = (f32[192]{0:T(256)S(1)}, f32[192]{0:T(256)}, u32[]{:S(2)}) copy-start(f32[192]{0:T(256)} %param.10) | copy-start | bytes 2308

commit v4 on v3

--- a/solution.py
+++ b/solution.py
@@ -138,6 +138,10 @@
             def _():
                 hop_right(h, part, s).start()
 
+            @pl.when(s >= 2)
+            def _():
+                hop_right(h, part, s - 2).wait_send()
+
     def land_left(t):
         s, h, part = piece(t)
         hop_left(h, part, s - 1).wait_recv()
@@ -146,11 +150,15 @@
         def _():
             hop_left(h, part, s).start()
 
+        @pl.when(s >= 2)
+        def _():
+            hop_left(h, part, s - 2).wait_send()
+
     def attend_right(t):
         u = t - lead
         s, h, part = piece(u)
 
-        @pl.when((u >= 0) & (u < RIGHT_HOPS * 2 * HEADS) & (part == 1))
+        @pl.when((u >= 0) & (s < RIGHT_HOPS) & (part == 1))
         def _():
             update(h, kv[h, s], 0, 2 * TOK)
 
@@ -198,14 +206,16 @@
                 remote(ostat.at[h], ostat_in.at[h], y_send.at[4 + h], y_recv.at[4 + h], across))
 
     def last_step(h, carry):
-        def arrive(part, inner):
-            t = (LEFT_HOPS - 1) * 2 * HEADS + 2 * h + part
-            pass_on(t, 0)
-            attend_right(t)
-            return inner
-
-        lax.fori_loop(0, 2, arrive, 0)
-        block = kv[h, RING - LEFT_HOPS]
+        def last_rows(part):
+            rows = pl.ds(part * HALF, HALF)
+            return jnp.concatenate(
+                [kv[h, RIGHT_HOPS, rows], kv[h, RING - LEFT_HOPS, rows]], axis=0)
+
+        t = (LEFT_HOPS - 1) * 2 * HEADS + 2 * h
+        pass_on(t, 0)
+        update(h, last_rows(0), 0, 2 * TOK)
+        pass_on(t + 1, 0)
+        block = last_rows(1)
         update(h, block, TOK, TOK)
         cols = pl.ds(TOK, TOK)
         total = acc[h, pl.ds(0, 8), cols][0:1]
@@ -217,22 +227,7 @@
         update(h, block, 0, TOK)
         return carry
 
-    ostat[...] = jnp.zeros_like(ostat)
     lax.fori_loop(0, HEADS, last_step, 0)
-
-    def sent(t, carry):
-        s, h = t // HEADS, t % HEADS
-        for part in range(2):
-            hop_left(h, part, s).wait_send()
-
-            @pl.when(s < RIGHT_HOPS)
-            def _():
-                hop_right(h, part, s).wait_send()
-
-        return carry
-
-    lax.fori_loop(0, LEFT_HOPS * HEADS, sent, 0)
-    q_move.wait_send()
 
     def g_move(h, j):
         return remote(att.at[h, head], att.at[h, head], g_send.at[h, j], g_recv.at[h, j], plane(j))
@@ -261,11 +256,15 @@
 
     lax.fori_loop(0, HEADS, combine, 0)
 
+    def sent(t, carry):
+        hop_right(t // 2, t % 2, RIGHT_HOPS - 1).wait_send()
+        hop_left(t // 2, t % 2, LEFT_HOPS - 1).wait_send()
+        return carry
+
+    lax.fori_loop(0, 2 * HEADS, sent, 0)
+    q_move.wait_send()
+
     def drain(h):
-        for move in o_moves(h):
-            move.wait_send()
-        for j in range(1, 8):
-            g_move(h, j).wait_send()
         for j in range(8):
             c_move(h, j).wait_send()
 
@@ -277,6 +276,10 @@
         for j in (1, 3, 4, 2, 5, 7, 6):
             g_move(h, j).wait_recv()
             c_move(h, j).start()
+        for j in range(1, 8):
+            g_move(h, j).wait_send()
+        for move in o_moves(h):
+            move.wait_send()
         for j in range(8):
             c_move(h, j).wait_recv()
         part = jnp.dot(wp[h], att[h].reshape(16 * HD, TOK), preferred_element_type=jnp.float32)
@@ -309,9 +312,9 @@
             pltpu.VMEM((HEADS, ROWS, 2 * TOK), f32),
             pltpu.VMEM((HEADS, 1, 2 * TOK), f32),
             pltpu.VMEM((HEADS, HD, TOK), bf16),
-            pltpu.VMEM((HEADS, 8, TOK), f32),
+            pltpu.VMEM((HEADS, 2, TOK), f32),
             pltpu.VMEM((HEADS, HD, TOK), bf16),
-            pltpu.VMEM((HEADS, 8, TOK), f32),
+            pltpu.VMEM((HEADS, 2, TOK), f32),
             pltpu.VMEM((HEADS, 16, HD, TOK), bf16),
             dma((4,)),
             dma((2, HEADS, 2, LEFT_HOPS)),

time: 64.5 us -> 64 us (level)
  Pallas kernels: 63.5 us -> 62.8 us
    pallas_call x1, Pallas kernels: 63.5 us -> 62.8 us  [on_device(): pl.pallas_call(fused, out_shape=jax.ShapeDtypeStruct((HEADS * HD, TOK), f...]
where the time goes in v4:
time: 64 us; the launch traced here: 63.6 us
  Pallas kernels  62.8 us (98%)
  other arithmetic  0.74 us (1%)
    pallas_call x1, Pallas kernels, on_device(): pl.pallas_call(fused, out_shape=jax.ShapeDtypeStruct((HEADS * HD, TOK), f...  62.8 us

profile of v4, /device:TPU:1, one launch (start us, length us, event | category | flops | bytes accessed | tf_op | source)
XLA Modules:
  0.0 63.6 jit_solution(1461455278746089761)
XLA Ops:
  0.0 0.0 copy-start
  0.0 0.0 copy-start.1
  0.0 62.8 %shard_map.64 = f32[192,256]{1,0:T(8,128)S(1)} custom-call(bf16[192,256]{1,0:T(8,128)(2,1)} %q_in.1, bf16[3,256,128]{2,1,0:T(8,128)(2,1)} %bitcast.2, bf16[3,256,128]{2,1,0:T(8,128)(2,1)} %bitcast.3, bf16[192,3072]{1,0:T(8,128)(2,1)} %w_in.1), custom_call_target="tpu_custom_call" | custom-call | flops 2000000000 | bytes 4000000 | tf_op jit(solution)/shard_map/pallas_call | solution.py:299
  62.8 0.0 copy-done
  62.8 0.0 copy-done.1
  62.8 0.7 %add_convert_fusion = bf16[192,256]{1,0:T(8,128)(2,1)} fusion(f32[192,256]{1,0:T(8,128)S(1)} %shard_map.64, bf16[192,256]{1,0:T(8,128)(2,1)S(1)} %copy-done, f32[192]{0:T(256)S(1)} %copy-done.1), kind=kLoop, calls=%fused_computation | loop fusion | flops 196608 | bytes 393984 | tf_op jit(solution)/shard_map/convert_element_type | solution.py:335
Async XLA Ops:
  0.0 62.8 %copy-start = (bf16[192,256]{1,0:T(8,128)(2,1)S(1)}, bf16[192,256]{1,0:T(8,128)(2,1)}, u32[]{:S(2)}) copy-start(bf16[192,256]{1,0:T(8,128)(2,1)} %param.9) | copy-start | bytes 294916
  0.0 62.8 %copy-start.1 = (f32[192]{0:T(256)S(1)}, f32[192]{0:T(256)}, u32[]{:S(2)}) copy-start(f32[192]{0:T(256)} %param.10) | copy-start | bytes 2308

commit v5 on v4

--- a/solution.py
+++ b/solution.py
@@ -170,8 +170,8 @@
             update(h, kv[h, RING - s], 0, 2 * TOK)
 
     def pass_on(t, carry):
+        land_left(t)
         land_right(t)
-        land_left(t)
         return carry
 
     lax.fori_loop(0, HEADS, pass_on, 0)
@@ -186,8 +186,8 @@
     lax.fori_loop(0, HEADS, own_stale, 0)
 
     def ring_step(t, carry):
+        land_left(t)
         land_right(t)
-        land_left(t)
         attend_right(t)
         attend_left(t)
         late = t // 4 - 1
@@ -249,7 +249,7 @@
         mixed = (acc[h, pl.ds(16, HD), cols] * (scale_a * inverse)
                  + oin[h].astype(jnp.float32) * (total_b * inverse))
         att[h, head] = mixed.astype(jnp.bfloat16)
-        for j in (1, 3, 4, 2, 5, 7, 6):
+        for j in (2, 1, 3, 6, 5, 7, 4):
             g_move(h, j).start()
         c_move(h, 0).start()
         return carry
@@ -273,7 +273,7 @@
         def _():
             drain(h - 1)
 
-        for j in (1, 3, 4, 2, 5, 7, 6):
+        for j in (2, 1, 3, 6, 5, 7, 4):
             g_move(h, j).wait_recv()
             c_move(h, j).start()
         for j in range(1, 8):

time: 64 us -> 63.7 us (level)
  no operation moved by 1% of the time
where the time goes in v5:
time: 63.7 us; the launch traced here: 63.6 us
  Pallas kernels  62.8 us (99%)
  other arithmetic  0.74 us (1%)
    pallas_call x1, Pallas kernels, on_device(): pl.pallas_call(fused, out_shape=jax.ShapeDtypeStruct((HEADS * HD, TOK), f...  62.8 us

profile of v5, /device:TPU:1, one launch (start us, length us, event | category | flops | bytes accessed | tf_op | source)
XLA Modules:
  0.0 63.6 jit_solution(7270651093914724305)
XLA Ops:
  0.0 0.0 copy-start
  0.0 0.0 copy-start.1
  0.0 62.8 %shard_map.64 = f32[192,256]{1,0:T(8,128)S(1)} custom-call(bf16[192,256]{1,0:T(8,128)(2,1)} %q_in.1, bf16[3,256,128]{2,1,0:T(8,128)(2,1)} %bitcast.2, bf16[3,256,128]{2,1,0:T(8,128)(2,1)} %bitcast.3, bf16[192,3072]{1,0:T(8,128)(2,1)} %w_in.1), custom_call_target="tpu_custom_call" | custom-call | flops 2000000000 | bytes 4000000 | tf_op jit(solution)/shard_map/pallas_call | solution.py:299
  62.9 0.0 copy-done
  62.9 0.0 copy-done.1
  62.9 0.7 %add_convert_fusion = bf16[192,256]{1,0:T(8,128)(2,1)} fusion(f32[192,256]{1,0:T(8,128)S(1)} %shard_map.64, bf16[192,256]{1,0:T(8,128)(2,1)S(1)} %copy-done, f32[192]{0:T(256)S(1)} %copy-done.1), kind=kLoop, calls=%fused_computation | loop fusion | flops 196608 | bytes 393984 | tf_op jit(solution)/shard_map/convert_element_type | solution.py:335
Async XLA Ops:
  0.0 62.9 %copy-start = (bf16[192,256]{1,0:T(8,128)(2,1)S(1)}, bf16[192,256]{1,0:T(8,128)(2,1)}, u32[]{:S(2)}) copy-start(bf16[192,256]{1,0:T(8,128)(2,1)} %param.9) | copy-start | bytes 294916
  0.0 62.9 %copy-start.1 = (f32[192]{0:T(256)S(1)}, f32[192]{0:T(256)}, u32[]{:S(2)}) copy-start(f32[192]{0:T(256)} %param.10) | copy-start | bytes 2308
